TPU v7x, 32 devices: a whole 2x2x4 slice. The times are simulated.
32 devices in a mesh: groups: 2 (over y), atoms: 4 (over z), kvec: 2 (over x), rep: 2 (over core).
Axes of the slice: x: 2, y: 2, z: 4, core: 2. Of those that a mesh axis runs over, the one named last changes fastest.
Arguments:
- positions: float32 [4, 3, 8192], P(('groups', 'rep'), None, 'atoms'), parts along dimension 0, may hold values from 0 to 1
- features: bfloat16 [4, 8192, 256], P(('groups', 'rep'), 'atoms'), parts along dimension 0
- species: int32 [4, 8192], P(('groups', 'rep'), 'atoms'), parts along dimension 0, may hold values from 0 to 7
- cell_length: float32 [4], P(('groups', 'rep')), parts along dimension 0, may hold values from 40 to 60
- energy_ref: float32 [4], P(('groups', 'rep')), parts along dimension 0, may hold values from -12 to -6
- miller_index: int32 [3, 2048], P(None, 'kvec'), may hold values from -8 to 8, as said below
- weight_in: bfloat16 [256, 512], replicated, may hold values from -0.375 to 0.375
- weight_mid: bfloat16 [512, 512], replicated, may hold values from -0.25 to 0.25
- weight_out: bfloat16 [512, 32], replicated, may hold values from -0.25 to 0.25
- species_bias: float32 [8, 512], replicated, may hold values from -3 to 3
Outputs:
- potential: float32 [4, 8192, 32], P(('groups', 'rep'), ('atoms', 'kvec')), parts along dimension 0
- energy: float32 [4], P(('groups', 'rep')), parts along dimension 0
- grad_in: float32 [512, 512], P('groups'), parts along dimension 0
- grad_mid: float32 [1024, 512], P('groups'), parts along dimension 0
- grad_out: float32 [1024, 32], P('groups'), parts along dimension 0
- grad_bias: float32 [16, 512], P('groups'), parts along dimension 0
There are 2 independent parts, one for each index of `groups`. A program takes and returns all parts, laid end to end along the dimension named above; an argument that names none is the same for every part. Nothing has to cross between parts.
Inputs may be any that keep to these rules, and one draw needn't show every extreme that they name: No column of miller_index is all zeros.
All inputs are finite; a program needn't handle non-finite values.
Results may differ from a plain program's by a relative error of at most 0.0046.
Values may be sent and summed in bfloat16 or wider, within the bound.
A program may use at most 64 MiB of HBM per device.

v0:
```python
import math

import jax
import jax.numpy as jnp
from jax import lax
from jax.sharding import PartitionSpec as P

KVECS = 2048


TWO_PI = 2.0 * math.pi
HIGHEST = lax.Precision.HIGHEST


def phase_tiles(coord_rows, miller_float):
    phase_turns = (
        coord_rows[0][:, None] * miller_float[0][None, :]
        + coord_rows[1][:, None] * miller_float[1][None, :]
        + coord_rows[2][:, None] * miller_float[2][None, :]
    )
    phase_angle = TWO_PI * phase_turns
    return jnp.concatenate([jnp.cos(phase_angle), jnp.sin(phase_angle)], axis=1).astype(
        jnp.bfloat16
    )


def wave_weights(miller_float, cell_size, atoms_total):
    index_square = (
        miller_float[0] * miller_float[0]
        + miller_float[1] * miller_float[1]
        + miller_float[2] * miller_float[2]
    )
    factor = TWO_PI / cell_size
    wave_square = index_square * (factor * factor)
    decay_base = jnp.exp(-0.5 * wave_square) / wave_square * (1.0 / math.sqrt(atoms_total * KVECS))
    return jnp.concatenate([decay_base, decay_base])


def contract_rows(left_rows, right_rows):
    return lax.dot_general(
        left_rows, right_rows, (((0,), (0,)), ((), ())), preferred_element_type=jnp.float32
    )


def silu_slope(linear):
    sigmoid_value = jax.nn.sigmoid(linear)
    return sigmoid_value * (1.0 + linear * (1.0 - sigmoid_value))


def forward(atom_features, atom_species, weight_in, weight_mid, weight_out, species_bias):
    kinds = jnp.arange(species_bias.shape[0], dtype=jnp.int32)
    onehot = (atom_species[:, None] == kinds[None, :]).astype(jnp.float32)
    bias_rows = jnp.dot(onehot, species_bias, precision=HIGHEST, preferred_element_type=jnp.float32)
    linear_one = jnp.dot(atom_features, weight_in, preferred_element_type=jnp.float32) + bias_rows
    hidden_one = jax.nn.silu(linear_one).astype(jnp.bfloat16)
    linear_two = jnp.dot(hidden_one, weight_mid, preferred_element_type=jnp.float32)
    hidden_two = jax.nn.silu(linear_two).astype(jnp.bfloat16)
    charges = jnp.dot(hidden_two, weight_out, preferred_element_type=jnp.float32).astype(
        jnp.bfloat16
    )
    return (onehot, linear_one, hidden_one, linear_two, hidden_two, charges)


def backward(
    atom_features,
    onehot,
    linear_one,
    hidden_one,
    linear_two,
    hidden_two,
    grad_charges,
    weight_mid,
    weight_out,
):
    grad_out = contract_rows(hidden_two, grad_charges)
    back_two = lax.dot_general(
        grad_charges, weight_out, (((1,), (1,)), ((), ())), preferred_element_type=jnp.float32
    )
    grad_two = (back_two * silu_slope(linear_two)).astype(jnp.bfloat16)
    grad_mid = contract_rows(hidden_one, grad_two)
    back_one = lax.dot_general(
        grad_two, weight_mid, (((1,), (1,)), ((), ())), preferred_element_type=jnp.float32
    )
    grad_one = (back_one * silu_slope(linear_one)).astype(jnp.bfloat16)
    grad_in = contract_rows(atom_features, grad_one)
    grad_bias = contract_rows(onehot.astype(jnp.bfloat16), grad_one)
    return (grad_in, grad_mid, grad_out, grad_bias)


def body(
    positions,
    features,
    species,
    cell_length,
    energy_ref,
    miller_index,
    weight_in,
    weight_mid,
    weight_out,
    species_bias,
):
    block_rows = positions.shape[2]
    kvec_count = miller_index.shape[1]
    channels = weight_out.shape[1]
    atoms_total = block_rows * lax.axis_size("atoms")
    quarter = block_rows // lax.axis_size("kvec")
    own_first = lax.axis_index("kvec") * quarter
    miller_float = miller_index.astype(jnp.float32)
    column_weights = wave_weights(miller_float, cell_length[0], atoms_total)
    coords = positions[0]
    step_rows = math.gcd(block_rows, 512)
    stored = jnp.concatenate(
        [
            phase_tiles(lax.slice_in_dim(coords, offset, offset + step_rows, axis=1), miller_float)
            for offset in range(0, block_rows, step_rows)
        ],
        axis=0,
    )

    def tile_rows(first_row, row_count):
        return lax.dynamic_slice_in_dim(stored, first_row, row_count, 0)

    zero_panels = jnp.zeros((channels, 2 * kvec_count), jnp.float32)
    own_features = features[0]
    own_species = species[0]
    onehot, linear_one, hidden_one, linear_two, hidden_two, charges = forward(
        own_features, own_species, weight_in, weight_mid, weight_out, species_bias
    )
    running = zero_panels
    row_count = charges.shape[0]
    piece_rows = math.gcd(row_count, 512)
    for inner_start in range(0, row_count, piece_rows):
        phase_rows = tile_rows(0 + inner_start, piece_rows)
        running = running + contract_rows(
            lax.slice_in_dim(charges, inner_start, inner_start + piece_rows, axis=0), phase_rows
        )
    summed = lax.psum(running, "atoms")
    energy_sum = lax.psum(jnp.sum(summed * summed * column_weights[None, :]).reshape(1), "kvec")
    weighted = (summed * column_weights[None, :]).astype(jnp.bfloat16)
    energy = energy_sum / atoms_total
    piece_rows = math.gcd(block_rows, 512)
    pieces = []
    for inner_start in range(0, block_rows, piece_rows):
        phase_rows = tile_rows(0 + inner_start, piece_rows)
        pieces.append(
            lax.dot_general(
                phase_rows, weighted, (((1,), (1,)), ((), ())), preferred_element_type=jnp.float32
            )
        )
    used_potential = lax.psum(jnp.concatenate(pieces, axis=0), "kvec")
    own_potential = lax.dynamic_slice_in_dim(used_potential, own_first, quarter, 0)
    loss_scale = (energy[0] - energy_ref[0]) * (2.0 / atoms_total)
    grad_charges = (loss_scale * used_potential).astype(jnp.bfloat16)
    local_in, local_mid, local_out, local_bias = backward(
        own_features,
        onehot,
        linear_one,
        hidden_one,
        linear_two,
        hidden_two,
        grad_charges,
        weight_mid,
        weight_out,
    )
    grad_in, grad_mid, grad_out, grad_bias = lax.psum(
        (local_in, local_mid, local_out, local_bias), ("atoms", "rep")
    )
    return (own_potential[None], energy, grad_in, grad_mid, grad_out, grad_bias)


def solution(mesh):
    placed = (
        P(("groups", "rep"), None, "atoms"),
        P(("groups", "rep"), "atoms", None),
        P(("groups", "rep"), "atoms"),
        P(("groups", "rep")),
        P(("groups", "rep")),
        P(None, "kvec"),
        P(),
        P(),
        P(),
        P(),
    )
    return jax.shard_map(
        body,
        mesh=mesh,
        in_specs=placed,
        out_specs=(
            P(("groups", "rep"), ("atoms", "kvec"), None),
            P(("groups", "rep")),
            P("groups", None),
            P("groups", None),
            P("groups", None),
            P("groups", None),
        ),
        check_vma=False,
    )
```

profile of v0, /device:TPU:0, one launch (start us, length us, event | category | flops | bytes accessed | tf_op | source)
XLA Modules:
  0.0 213.0 jit_solution(59138224484041995)
XLA Ops:
  7.2 0.8 convert_element_type.34
  8.0 0.8 copy.19
  8.9 1.7 fusion.6
  10.6 4.2 %multiply_convert_fusion.3 = (bf16[2048,512]{1,0:T(8,128)(2,1)S(1)}, f32[2048,512]{1,0:T(8,128)}) fusion(f32[2048,512]{1,0:T(8,128)S(1)} %fusion.6, f32[8,512]{1,0:T(8,128)S(1)} %copy-done.19, s32[2048]{0:T(1024)S(1)} %bitcast.56), kind=kOutput, calls=%fused_computation.4 | convolution fusion | flops 106971136 | bytes 10510336 | tf_op jit(solution)/shard_map/dot_general | solution.py:53
  14.8 3.8 %multiply_convert_fusion.2 = (bf16[2048,512]{1,0:T(8,128)(2,1)S(1)}, f32[2048,512]{1,0:T(8,128)}) fusion(bf16[2048,512]{1,0:T(8,128)(2,1)S(1)} %get-tuple-element.46, bf16[512,512]{1,0:T(8,128)(2,1)S(1)} %copy-done.17), kind=kOutput, calls=%fused_computation.2 | convolution fusion | flops 1078984704 | bytes 8912896 | tf_op jit(solution)/shard_map/dot_general | solution.py:56
  19.2 33.6 %cosine_convert_fusion = (bf16[512,1024]{1,0:T(8,128)(2,1)S(1)}, bf16[512,1024]{1,0:T(8,128)(2,1)S(1)}, bf16[512,1024]{1,0:T(8,128)(2,1)S(1)}, bf16[512,1024]{1,...) fusion(f32[512]{0:T(512)S(1)} %bitcast.59, ...), kind=kLoop, calls=%fused_computation.16 | loop fusion | flops 16777216 | bytes 8425472 | tf_op jit(solution)/shard_map/convert
  55.5 1.2 convolution_add_fusion.1
  57.5 37.4 %all-reduce.5.cloned.1.call-done = f32[32,2048]{1,0:T(8,128)} async-done(((f32[32,2048]{1,0:T(8,128)}), f32[32,2048]{1,0:T(8,128)}) %all-reduce.5.cloned.1.call-update) | async-done | bytes 262160 | tf_op jit(solution)/shard_map/psum | solution.py:137
  94.8 1.8 multiply_reduce_fusion
  96.6 2.3 %fusion = f32[512,32]{0,1:T(8,128)S(1)} fusion(bf16[32,2048]{1,0:T(8,128)(2,1)S(1)} %get-tuple-element.16, bf16[512,1024]{1,0:T(8,128)(2,1)} %copy-done.12, bf16[512,1024]{1,0:T(8,128)(2,1)} %copy-done.11), kind=kOutput, calls=%fused_computation.27 | convolution fusion | flops 71303168 | bytes 2293760 | tf_op jit(solution)/shard_map/dot_general | solution.py:146
  100.4 0.7 fusion.2
  101.9 0.7 pad_maximum_fusion.12
  103.4 5.6 %psum.51 = f32[1]{0:T(128)} all-reduce(f32[1]{0:T(128)} %bitcast.19), channel_id=1, replica_groups=mesh['groups'=2,'atoms'=4,'kvec'=2,'rep'=2] {'kvec'}, use_global_device_ids=true, to_apply=%region_3.4 | all-reduce | flops 1 | bytes 8 | tf_op jit(solution)/shard_map/psum | solution.py:138
  109.6 16.1 %all-reduce.7.cloned.1.call-done = f32[2048,32]{0,1:T(8,128)} async-done(((f32[2048,32]{0,1:T(8,128)}), f32[2048,32]{0,1:T(8,128)}) %all-reduce.7.cloned.1.call-update) | async-done | bytes 262160 | tf_op jit(solution)/shard_map/psum | solution.py:150
  125.8 4.2 %multiply_convert_fusion.1 = bf16[2048,512]{1,0:T(8,128)(2,1)S(1)} fusion(f32[2048,512]{1,0:T(8,128)} %get-tuple-element.49, bf16[512,32]{0,1:T(8,128)(2,1)S(1)} %copy-done.15, f32[2048,32]{0,1:T(8,128)} %all-reduce.7.cloned.1.call-done, f32[]{:T(128)} %bitcast.20), kind=kOutput, calls=%fused_computation.1 | convolution fusion | flops 76677120 | bytes 6586372 | tf_op jit(solution)/shard_map/dot_general | solution.py:76
  130.0 2.3 %fusion.26 = f32[512,512]{1,0:T(8,128)} fusion(bf16[2048,512]{1,0:T(8,128)(2,1)S(1)} %copy-done.21, bf16[2048,512]{1,0:T(8,128)(2,1)S(1)} %multiply_convert_fusion.1), kind=kOutput, calls=%fused_computation.64 | convolution fusion | flops 1073741824 | bytes 5242880 | tf_op jit(solution)/shard_map/dot_general | solution.py:40
  132.5 2.3 %multiply_convert_fusion = bf16[2048,512]{1,0:T(8,128)(2,1)S(1)} fusion(f32[2048,512]{1,0:T(8,128)S(1)} %copy-done.22, bf16[2048,512]{1,0:T(8,128)(2,1)S(1)} %multiply_convert_fusion.1, bf16[512,512]{1,0:T(8,128)(2,1)S(1)} %copy-done.18), kind=kOutput, calls=%fused_computation | convolution fusion | flops 1083179008 | bytes 8912896 | tf_op jit(solution)/shard_map/dot_general | solution.py:81
  134.9 1.5 convolution_bitcast_fusion
  136.5 1.1 fusion.11
  137.6 0.8 fusion.8
  138.4 29.5 %psum.55 = f32[8,512]{1,0:T(8,128)} all-reduce(f32[8,512]{1,0:T(8,128)S(1)} %fusion.8), channel_id=1, replica_groups=mesh['groups'=2,'atoms'=4,'kvec'=2,'rep'=2] {'atoms','rep'}, use_global_device_ids=true, to_apply=%region_7.8 | all-reduce | flops 4096 | bytes 32768 | tf_op jit(solution)/shard_map/psum | solution.py:165
  168.6 31.8 %all-reduce.9.cloned.1.call-done = (f32[256,512]{0,1:T(8,128)}, f32[512,512]{1,0:T(8,128)}, f32[512,32]{0,1:T(8,128)}) async-done(((f32[256,512]{0,1:T(8,128)}, f32[512,512]{1,0:T(8,128)}, f32[512,32]{0,1:T(8,128)}), (f32[256,512]{0,1:T(8,128)}, f32[512,512]{1,0:T(8,128)}, f32[512,32]{0,1:T(8,128)})) %all-reduce.9.cloned.1.call-update) | async-done | bytes 1638416 | tf_op jit(solution)/shard_map/psum | solution.py:165
  200.3 2.1 copy.16
  202.4 2.3 %copy.27 = f32[512,512]{1,0:T(8,128)} copy(f32[512,512]{1,0:T(8,128)} %get-tuple-element.53) | data formatting | bytes 2097152
  (64 shorter events, 7.5 us)
Async XLA Ops:
  7.2 1.7 copy-start
  7.2 87.7 %all-reduce.5.cloned.1.call-start = ((), (), s32[]{:S(2)}) async-start(), calls=%async_computation | async-start | bytes 524288 | tf_op jit(solution)/shard_map/psum | solution.py:137
  8.8 1.7 copy-start.16
  8.8 1.7 copy-start.19
  10.6 4.2 %copy-start.17 = (bf16[512,512]{1,0:T(8,128)(2,1)S(1)}, bf16[512,512]{1,0:T(8,128)(2,1)}, u32[]{:S(2)}) copy-start(bf16[512,512]{1,0:T(8,128)(2,1)} %param.17) | copy-start | bytes 1572868
  14.8 3.8 %copy-start.20 = (bf16[2048,512]{1,0:T(8,128)(2,1)}, bf16[2048,512]{1,0:T(8,128)(2,1)S(1)}, u32[]{:S(2)}) copy-start(bf16[2048,512]{1,0:T(8,128)(2,1)S(1)} %get-tuple-element.46) | copy-start | bytes 6291460
  14.8 3.8 %copy-start.15 = (bf16[512,32]{0,1:T(8,128)(2,1)S(1)}, bf16[512,32]{0,1:T(8,128)(2,1)}, u32[]{:S(2)}) copy-start(bf16[512,32]{0,1:T(8,128)(2,1)} %param.18) | copy-start | bytes 98308
  18.5 34.3 %copy-start.1 = (bf16[2048,512]{1,0:T(8,128)(2,1)}, bf16[2048,512]{1,0:T(8,128)(2,1)S(1)}, u32[]{:S(2)}) copy-start(bf16[2048,512]{1,0:T(8,128)(2,1)S(1)} %get-tuple-element.48) | copy-start | bytes 6291460
  52.8 1.3 copy-start.5
  52.8 1.6 copy-start.7
  52.9 1.9 copy-start.9
  52.9 2.4 %copy-start.11 = (bf16[512,1024]{1,0:T(8,128)(2,1)}, bf16[512,1024]{1,0:T(8,128)(2,1)S(1)}, u32[]{:S(2)}) copy-start(bf16[512,1024]{1,0:T(8,128)(2,1)S(1)} %get-tuple-element.29) | copy-start | bytes 3145732
  52.9 2.6 %copy-start.12 = (bf16[512,1024]{1,0:T(8,128)(2,1)}, bf16[512,1024]{1,0:T(8,128)(2,1)S(1)}, u32[]{:S(2)}) copy-start(bf16[512,1024]{1,0:T(8,128)(2,1)S(1)} %get-tuple-element.30) | copy-start | bytes 3145732
  56.7 69.1 %all-reduce.7.cloned.1.call-start = ((), (), s32[]{:S(2)}) async-start(), calls=%async_computation.1 | async-start | bytes 524288 | tf_op jit(solution)/shard_map/psum | solution.py:150
  94.8 4.1 %copy-start.8 = (bf16[512,1024]{1,0:T(8,128)(2,1)S(1)}, bf16[512,1024]{1,0:T(8,128)(2,1)}, u32[]{:S(2)}) copy-start(bf16[512,1024]{1,0:T(8,128)(2,1)} %copy-done.7) | copy-start | bytes 3145732
  94.8 4.1 %copy-start.10 = (bf16[512,1024]{1,0:T(8,128)(2,1)S(1)}, bf16[512,1024]{1,0:T(8,128)(2,1)}, u32[]{:S(2)}) copy-start(bf16[512,1024]{1,0:T(8,128)(2,1)} %copy-done.9) | copy-start | bytes 3145732
  98.9 1.5 copy-start.6
  102.7 97.7 %all-reduce.9.cloned.1.call-start = ((), (), s32[]{:S(2)}) async-start(), calls=%async_computation.2 | async-start | bytes 3276800 | tf_op jit(solution)/shard_map/psum | solution.py:165
  125.8 4.2 %copy-start.21 = (bf16[2048,512]{1,0:T(8,128)(2,1)S(1)}, bf16[2048,512]{1,0:T(8,128)(2,1)}, u32[]{:S(2)}) copy-start(bf16[2048,512]{1,0:T(8,128)(2,1)} %copy-done.20) | copy-start | bytes 6291460
  129.9 2.3 %copy-start.18 = (bf16[512,512]{1,0:T(8,128)(2,1)S(1)}, bf16[512,512]{1,0:T(8,128)(2,1)}, u32[]{:S(2)}) copy-start(bf16[512,512]{1,0:T(8,128)(2,1)} %param.17) | copy-start | bytes 1572868
  130.0 2.6 %copy-start.22 = (f32[2048,512]{1,0:T(8,128)S(1)}, f32[2048,512]{1,0:T(8,128)}, u32[]{:S(2)}) copy-start(f32[2048,512]{1,0:T(8,128)} %get-tuple-element.47) | copy-start | bytes 12582916
  134.9 1.6 copy-start.2
  134.9 1.6 copy-start.13
  200.3 4.3 %copy-start.14 = (f32[512,32]{0,1:T(8,128)S(1)}, f32[512,32]{0,1:T(8,128)}, u32[]{:S(2)}) copy-start(f32[512,32]{0,1:T(8,128)} %get-tuple-element.54) | copy-start | bytes 196612
  (2 other events, 2.3 us)
Sparse Core Ops, SparseCore 0:
  56.8 37.9 all-reduce.4
  102.8 22.9 all-reduce.6
  137.7 62.5 all-reduce.8
where the time goes:
time: 213 us
  waiting for transfers between devices  85.4 us (40%)
  other arithmetic  36.9 us (17%)
  blocking collectives  35.1 us (16%)
  matrix products  29.5 us (14%)
  between operations  17.1 us (8%)
  local copies, waits for them, and re-layouts  8.84 us (4%)
    psum x1, waiting for transfers between devices, body(): summed = lax.psum(running, 'atoms')  37.4 us
    another operation x1, other arithmetic  33.6 us
    psum x1, waiting for transfers between devices, body(): lax.psum((local_in, local_mid, local_out, local_bias), ('atoms', 'rep'))  31.8 us
    psum x1, blocking collectives, body(): lax.psum((local_in, local_mid, local_out, local_bias), ('atoms', 'rep'))  29.5 us
    psum x1, waiting for transfers between devices, body(): used_potential = lax.psum(jnp.concatenate(pieces, axis=0), 'kvec')  16.1 us
    dot_general x8, matrix products, contract_rows(): lax.dot_general(left_rows, right_rows, (((0,), (0,)), ((), ())), preferre...  8.23 us
    unnamed x50, local copies, waits for them, and re-layouts  8.15 us
    psum x1, blocking collectives, body(): lax.psum(jnp.sum(summed * summed * column_weights[None, :]).reshape(1), '...  5.58 us
  transfers between devices with their start and end apart: 3, of which 3 were waited for; matrix products, arithmetic and copies ran while one was open for 1% of the time, Pallas kernels for 0%

commit v1 on v0

--- a/solution.py
+++ b/solution.py
@@ -1,8 +1,11 @@
+import functools
 import math
 
 import jax
 import jax.numpy as jnp
 from jax import lax
+from jax.experimental import pallas as pl
+from jax.experimental.pallas import tpu as pltpu
 from jax.sharding import PartitionSpec as P
 
 KVECS = 2048
@@ -87,7 +90,7 @@
     return (grad_in, grad_mid, grad_out, grad_bias)
 
 
-def body(
+def plain_body(
     positions,
     features,
     species,
@@ -168,6 +171,368 @@
     return (own_potential[None], energy, grad_in, grad_mid, grad_out, grad_bias)
 
 
+TURN_SHIFT = 1.5 * 2.0**23
+SINE = (4.442867834, -7.307441175, 3.594769894, -0.784331973)
+COSINE = (1.414213496, -6.978850946, 5.739460314, -1.883557438, 0.310686957)
+ROWS = 256
+STRIP = 16
+BF = jnp.bfloat16
+F32 = jnp.float32
+
+
+def mul(left, right, dims):
+    return lax.dot_general(left, right, ((dims[:1], dims[1:]), ((), ())), preferred_element_type=F32)
+
+
+def split_three(value):
+    high = value.astype(BF).astype(F32)
+    rest = value - high
+    middle = rest.astype(BF).astype(F32)
+    return high, middle, rest - middle
+
+
+def fused(
+    nz, rows_b,
+    pos, feat, spec, clen, eref, mill, w_in, w_mid, w_out, bias,
+    pot_o, en_o, gin_o, gmid_o, gout_o, gbias_o,
+    pos_f, pos_s, mill_f, mill_s, bias_f, bias_s, hot, out_t, cw,
+    h1, h2, slope1, slope2, ch, turns, phases, panels,
+    pz_s, pz_r, w_all, en_mine, en_z, en_x, en_sum,
+    pot, pot_s, pot_r, gc, g2, g1,
+    ga, ra_s, ra_r, xa_s, xa_r, za_s, za_r, all_a,
+    gb, rb_s, rb_r, xb_s, xb_r, zb_s, zb_r, all_b,
+    send, recv,
+):
+    z = lax.axis_index("atoms")
+    x = lax.axis_index("kvec")
+    r = lax.axis_index("rep")
+    atoms = pos.shape[2]
+    half = atoms // 2
+    kv = mill.shape[1]
+    channels = w_out.shape[1]
+    width = 2 * kv // nz
+    atoms_total = atoms * nz
+    to_x = {"kvec": 1 - x}
+    to_r = {"rep": 1 - r}
+
+    def to_z(step):
+        return {"atoms": lax.rem(z + step, nz)}
+
+    barrier = pltpu.get_barrier_semaphore()
+    peers = [to_x, to_r] + [to_z(step) for step in range(1, nz)]
+    for peer in peers:
+        pl.semaphore_signal(barrier, inc=1, device_id=peer, device_id_type=pl.DeviceIdType.MESH)
+
+    count = [0]
+
+    def copy(src, dst, peer):
+        slot = count[0]
+        count[0] += 1
+        made = pltpu.make_async_remote_copy(
+            src_ref=src, dst_ref=dst, send_sem=send.at[slot], recv_sem=recv.at[slot],
+            device_id=peer, device_id_type=pl.DeviceIdType.MESH,
+        )
+        made.start()
+        return made
+
+    pos_f[...] = jnp.zeros_like(pos_f)
+    mill_f[...] = jnp.zeros_like(mill_f)
+    bias_f[...] = jnp.zeros_like(bias_f)
+    miller = mill[...].astype(F32)
+    for part, piece in enumerate(split_three(pos[0])):
+        pos_f[pl.ds(3 * part, 3), :] = piece
+        mill_f[pl.ds(3 * part, 3), :] = miller
+    pos_s[...] = pos_f[...].astype(BF)
+    mill_s[...] = mill_f[...].astype(BF)
+    for part, piece in enumerate(split_three(bias[...])):
+        bias_f[pl.ds(16 * part, bias.shape[0]), :] = piece
+    bias_s[...] = bias_f[...].astype(BF)
+    kinds = lax.rem(lax.broadcasted_iota(jnp.int32, hot.shape, 0), 16)
+    own_kind = jnp.broadcast_to(spec[:, pl.ds(pl.multiple_of(x * half, 128), half)], hot.shape)
+    hot[...] = (kinds == own_kind).astype(F32).astype(BF)
+    eye = (
+        lax.broadcasted_iota(jnp.int32, (channels, channels), 0)
+        == lax.broadcasted_iota(jnp.int32, (channels, channels), 1)
+    ).astype(F32).astype(BF)
+    out_t[...] = mul(eye, w_out[...], (1, 1)).astype(BF)
+    factor = TWO_PI / jnp.full((1, kv), clen[0], F32)
+    square = jnp.sum(miller * miller, axis=0, keepdims=True) * (factor * factor)
+    decay = jnp.exp(-0.5 * square) / square * (1.0 / math.sqrt(atoms_total * KVECS))
+    cw[:, pl.ds(0, kv)] = decay
+    cw[:, pl.ds(kv, kv)] = decay
+
+    @pl.loop(0, half // ROWS)
+    def _(i):
+        at = pl.ds(pl.multiple_of(i * ROWS, ROWS), ROWS)
+        source = pl.ds(pl.multiple_of(x * half + i * ROWS, ROWS), ROWS)
+        linear = mul(feat[0, source, :], w_in[...], (1, 0)) + mul(hot[:, at], bias_s[...], (0, 0))
+        gate = 0.5 * jnp.tanh(0.5 * linear) + 0.5
+        hidden = linear * gate
+        slope1[at, :] = gate + hidden * (1.0 - gate)
+        hidden = hidden.astype(BF)
+        h1[at, :] = hidden
+        linear = mul(hidden, w_mid[...], (1, 0))
+        gate = 0.5 * jnp.tanh(0.5 * linear) + 0.5
+        hidden = linear * gate
+        slope2[at, :] = gate + hidden * (1.0 - gate)
+        hidden = hidden.astype(BF)
+        h2[at, :] = hidden
+        ch[x, :, at] = mul(out_t[...], hidden, (1, 1)).astype(BF)
+
+    pl.semaphore_wait(barrier, len(peers))
+    charges = copy(ch.at[x], ch.at[x], to_x)
+
+    panels[...] = jnp.zeros_like(panels)
+
+    def phase_half(which):
+        @pl.loop(0, half // ROWS)
+        def _(i):
+            at = pl.ds(pl.multiple_of(i * ROWS, ROWS), ROWS)
+            base = pl.multiple_of(which * half + i * ROWS, ROWS)
+            turns[...] = mul(pos_s[:, pl.ds(base, ROWS)], mill_s[...], (0, 0))
+
+            @pl.loop(0, ROWS // STRIP, unroll=4)
+            def _(j):
+                near = turns[pl.ds(pl.multiple_of(j * STRIP, STRIP), STRIP), :]
+                near = near - ((near + TURN_SHIFT) - TURN_SHIFT)
+                sq = near * near
+                sine = near * (SINE[0] + sq * (SINE[1] + sq * (SINE[2] + sq * SINE[3])))
+                cosine = COSINE[0] + sq * (COSINE[1] + sq * (COSINE[2] + sq * (COSINE[3] + sq * COSINE[4])))
+                to = pl.ds(pl.multiple_of(base + j * STRIP, STRIP), STRIP)
+                phases[to, pl.ds(0, kv)] = (1.0 - sine * sine).astype(BF)
+                phases[to, pl.ds(kv, kv)] = (sine * cosine).astype(BF)
+
+            panels[...] += mul(ch[which, :, at], phases[pl.ds(base, ROWS), :], (1, 0))
+
+    phase_half(x)
+    charges.wait()
+    phase_half(1 - x)
+
+    def slab(who):
+        return pl.ds(pl.multiple_of(who * width, 128), width)
+
+    sums = []
+    for step in range(1, nz):
+        pz_s[step] = panels[:, slab(lax.rem(z + step, nz))].astype(BF)
+        sums.append(copy(pz_s.at[step], pz_r.at[step], to_z(step)))
+    for one in sums:
+        one.wait()
+    total = panels[:, slab(z)]
+    for step in range(1, nz):
+        total = total + pz_r[step].astype(F32)
+    weighed = total * cw[:, slab(z)]
+    w_all[z] = weighed.astype(BF)
+    en_mine[...] = jnp.broadcast_to(jnp.sum(total * weighed).reshape(1, 1), en_mine.shape)
+    gathers = []
+    for step in range(1, nz):
+        gathers.append(copy(w_all.at[z], w_all.at[z], to_z(step)))
+        gathers.append(copy(en_mine, en_z.at[step], to_z(step)))
+    for one in gathers:
+        one.wait()
+    energy = en_mine[...]
+    for step in range(1, nz):
+        energy = energy + en_z[step]
+    en_sum[...] = energy
+    energies = copy(en_sum, en_x, to_x)
+
+    def potential_half(which, store):
+        @pl.loop(0, half // ROWS)
+        def _(i):
+            at = pl.ds(pl.multiple_of(i * ROWS, ROWS), ROWS)
+            base = pl.ds(pl.multiple_of(which * half + i * ROWS, ROWS), ROWS)
+            value = mul(w_all[0], phases[base, pl.ds(0, width)], (1, 1))
+            for who in range(1, nz):
+                value = value + mul(w_all[who], phases[base, pl.ds(who * width, width)], (1, 1))
+            store[:, at] = value.astype(store.dtype)
+
+    potential_half(1 - x, pot_s)
+    others = copy(pot_s, pot_r, to_x)
+    potential_half(x, pot)
+    energies.wait()
+    others.wait()
+    energy = (en_sum[...] + en_x[...]) * (1.0 / atoms_total)
+    en_o[...] = energy
+    scale = (energy[0:1, 0:1] - eref[0]) * (2.0 / atoms_total)
+    full = pot[...] + pot_r[...].astype(F32)
+    pot[...] = full
+    gc[...] = (full * scale).astype(BF)
+
+    @pl.loop(0, half // ROWS)
+    def _(i):
+        at = pl.ds(pl.multiple_of(i * ROWS, ROWS), ROWS)
+        back = mul(gc[:, at], out_t[...], (0, 0))
+        g2[at, :] = (back * slope2[at, :]).astype(BF)
+
+    lanes = 128
+
+    def keep(store, first, value):
+        for block in range(4):
+            store[block, pl.ds(first, value.shape[0]), :] = value[:, block * lanes : (block + 1) * lanes]
+
+    for first in range(0, h1.shape[1], ROWS):
+        keep(ga, first, mul(h1[:, pl.ds(first, ROWS)], g2[...], (0, 0)))
+
+    mine = 2 * r + x
+
+    def rep_start(g, out, into):
+        out[...] = g[pl.ds(2 * (1 - r), 2)].astype(BF)
+        return copy(out, into, to_r)
+
+    def x_start(g, got, out, into):
+        out[...] = (g[2 * r + 1 - x] + got[1 - x].astype(F32)).astype(BF)
+        return copy(out, into, to_x)
+
+    def z_start(g, got_r, got_x, out, into):
+        total = g[mine] + got_r[x].astype(F32) + got_x[...].astype(F32)
+        g[mine] = total
+        out[...] = total.astype(BF)
+        share = out.shape[0] // nz
+        made = []
+        for step in range(1, nz):
+            piece = pl.ds(pl.multiple_of(lax.rem(z + step, nz) * share, 16), share)
+            made.append(copy(out.at[piece], into.at[step], to_z(step)))
+        return made
+
+    def z_gather(g, got, whole):
+        share = got.shape[1]
+        piece = pl.ds(pl.multiple_of(z * share, 16), share)
+        total = g[mine, piece, :]
+        for step in range(1, nz):
+            total = total + got[step].astype(F32)
+        whole[mine, piece, :] = total.astype(BF)
+        return [copy(whole.at[mine, piece], whole.at[mine, piece], to_z(step)) for step in range(1, nz)]
+
+    def finish(made):
+        for one in made:
+            one.wait()
+
+    rep_a = rep_start(ga, ra_s, ra_r)
+
+    @pl.loop(0, half // ROWS)
+    def _(i):
+        at = pl.ds(pl.multiple_of(i * ROWS, ROWS), ROWS)
+        back = mul(g2[at, :], w_mid[...], (1, 1))
+        g1[at, :] = (back * slope1[at, :]).astype(BF)
+
+    rep_a.wait()
+    x_a = x_start(ga, ra_r, xa_s, xa_r)
+    features_in = feat.shape[2]
+    own = pl.ds(pl.multiple_of(x * half, ROWS), half)
+    gb[...] = jnp.zeros_like(gb)
+    keep(gb, 0, mul(feat[0, own, :], g1[...], (0, 0)))
+    keep(gb, features_in, mul(gc[...], h2[...], (1, 0)))
+    keep(gb, features_in + channels, mul(hot[pl.ds(0, 16), :], g1[...], (1, 0)))
+    rep_b = rep_start(gb, rb_s, rb_r)
+    x_a.wait()
+    z_a = z_start(ga, ra_r, xa_r, za_s, za_r)
+    rep_b.wait()
+    x_b = x_start(gb, rb_r, xb_s, xb_r)
+    pot_o[...] = pot[...].T
+    finish(z_a)
+    all_z_a = z_gather(ga, za_r, all_a)
+    x_b.wait()
+    z_b = z_start(gb, rb_r, xb_r, zb_s, zb_r)
+    finish(all_z_a)
+    all_x_a = copy(all_a.at[mine], all_a.at[mine], to_x)
+    finish(z_b)
+    all_z_b = z_gather(gb, zb_r, all_b)
+    all_x_a.wait()
+    pair = pl.ds(2 * r, 2)
+    all_r_a = copy(all_a.at[pair], all_a.at[pair], to_r)
+    finish(all_z_b)
+    all_x_b = copy(all_b.at[mine], all_b.at[mine], to_x)
+    all_r_a.wait()
+    for block in range(4):
+        gmid_o[:, pl.ds(block * lanes, lanes)] = all_a[block].astype(F32)
+    all_x_b.wait()
+    all_r_b = copy(all_b.at[pair], all_b.at[pair], to_r)
+    all_r_b.wait()
+    for block in range(4):
+        at = pl.ds(block * lanes, lanes)
+        gin_o[:, at] = all_b[block, pl.ds(0, features_in), :].astype(F32)
+        gout_o[at, :] = all_b[block, pl.ds(features_in, channels), :].astype(F32).T
+        gbias_o[:, at] = all_b[block, pl.ds(features_in + channels, 16), :].astype(F32)[: gbias_o.shape[0]]
+
+
+def fits(sizes, args):
+    atoms, kv = args[0].shape[2], args[5].shape[1]
+    nz = sizes["atoms"]
+    return (
+        sizes["kvec"] == 2
+        and sizes["rep"] == 2
+        and nz > 1
+        and (2 * kv) % (128 * nz) == 0
+        and atoms % (2 * ROWS) == 0
+        and args[7].shape[0] % (16 * nz) == 0
+        and args[7].shape[1] == 512
+        and args[9].shape[0] <= 16
+    )
+
+
+def body(sizes, *args):
+    if not fits(sizes, args):
+        return plain_body(*args)
+    positions, features, _, _, _, miller_index, _, weight_mid, weight_out, species_bias = args
+    nz = sizes["atoms"]
+    atoms, kv = positions.shape[2], miller_index.shape[1]
+    half = atoms // 2
+    width = 2 * kv // nz
+    inner, channels = weight_out.shape
+    features_in = features.shape[2]
+    rows_a = inner
+    rows_b = -(-(features_in + channels + 16) // (16 * nz)) * 16 * nz
+
+    def vmem(*shape, dtype=F32):
+        return pltpu.VMEM(shape, dtype)
+
+    def grads(rows):
+        return [
+            vmem(4, rows, 128),
+            vmem(2, rows, 128, dtype=BF), vmem(2, rows, 128, dtype=BF),
+            vmem(rows, 128, dtype=BF), vmem(rows, 128, dtype=BF),
+            vmem(rows, 128, dtype=BF), vmem(nz, rows // nz, 128, dtype=BF),
+            vmem(4, rows, 128, dtype=BF),
+        ]
+
+    scratch = [
+        vmem(16, atoms), vmem(16, atoms, dtype=BF),
+        vmem(16, kv), vmem(16, kv, dtype=BF),
+        vmem(48, inner), vmem(48, inner, dtype=BF),
+        vmem(48, half, dtype=BF), vmem(channels, inner, dtype=BF), vmem(1, 2 * kv),
+        vmem(half, inner, dtype=BF), vmem(half, inner, dtype=BF),
+        vmem(half, inner), vmem(half, inner),
+        vmem(2, channels, half, dtype=BF), vmem(ROWS, kv), vmem(atoms, 2 * kv, dtype=BF),
+        vmem(channels, 2 * kv),
+        vmem(nz, channels, width, dtype=BF), vmem(nz, channels, width, dtype=BF),
+        vmem(nz, channels, width, dtype=BF),
+        vmem(8, 128), vmem(nz, 8, 128), vmem(8, 128), vmem(8, 128),
+        vmem(channels, half), vmem(channels, half, dtype=BF), vmem(channels, half, dtype=BF),
+        vmem(channels, half, dtype=BF), vmem(half, inner, dtype=BF), vmem(half, inner, dtype=BF),
+        *grads(rows_a), *grads(rows_b),
+        pltpu.SemaphoreType.DMA((48,)), pltpu.SemaphoreType.DMA((48,)),
+    ]
+    place = pl.BlockSpec(memory_space=pltpu.VMEM)
+    scalar = pl.BlockSpec(memory_space=pltpu.SMEM)
+    potential, energy, grad_in, grad_mid, grad_out, grad_bias = pl.pallas_call(
+        functools.partial(fused, nz, rows_b),
+        out_shape=(
+            jax.ShapeDtypeStruct((half, channels), F32),
+            jax.ShapeDtypeStruct((8, 128), F32),
+            jax.ShapeDtypeStruct((features_in, inner), F32),
+            jax.ShapeDtypeStruct((inner, inner), F32),
+            jax.ShapeDtypeStruct((inner, channels), F32),
+            jax.ShapeDtypeStruct(species_bias.shape, F32),
+        ),
+        in_specs=[place, place, place, scalar, scalar] + [place] * 5,
+        out_specs=[place] * 6,
+        scratch_shapes=scratch,
+        compiler_params=pltpu.CompilerParams(
+            collective_id=0, has_side_effects=True, vmem_limit_bytes=52 * 2**20
+        ),
+    )(*args)
+    return (potential[None], energy[0, :1], grad_in, grad_mid, grad_out, grad_bias)
+
+
 def solution(mesh):
     placed = (
         P(("groups", "rep"), None, "atoms"),
@@ -182,7 +547,7 @@
         P(),
     )
     return jax.shard_map(
-        body,
+        functools.partial(body, dict(mesh.shape)),
         mesh=mesh,
         in_specs=placed,
         out_specs=(

time: 213 us -> 71.6 us (0.34)
  waiting for transfers between devices: 85.4 us -> 0 us
  Pallas kernels: 0 us -> 62.3 us
  other arithmetic: 36.9 us -> 0 us
  blocking collectives: 35.1 us -> 0 us
  matrix products: 29.5 us -> 0 us
  between operations: 17.1 us -> 2 us
    psum x3 -> x0, waiting for transfers between devices: 85.3 us -> none  [the longest x1 37.4 us: body(): summed = lax.psum(running, 'atoms')]
    pallas_call x0 -> x1, Pallas kernels: none -> 62.3 us  [body(): pl.pallas_call(functools.partial(fused, nz, rows_b), out_shape=(jax.Shape...]
    psum x2 -> x0, blocking collectives: 35.1 us -> none  [the longest x1 29.5 us: body(): lax.psum((local_in, local_mid, local_out, local_bias), ('atoms', 'rep'))]
    another operation x1 -> x0, other arithmetic: 33.6 us -> none
    dot_general x18 -> x0, matrix products: 29.5 us -> none  [the longest x8 8.23 us: contract_rows(): lax.dot_general(left_rows, right_rows, (((0,), (0,)), ((), ())), preferre...]
    unnamed x50 -> x19, local copies, waits for them, and re-layouts: 8.15 us -> 6.36 us
  transfers between devices with their start and end apart: 3 -> 0, of which waited for: 3 -> 0; matrix products, arithmetic and copies ran while one was open for 1% -> 0% of each run, Pallas kernels for 0% -> 0%
where the time goes in v1:
time: 71.6 us; the launch traced here: 71.2 us
  Pallas kernels  62.3 us (87%)
  local copies, waits for them, and re-layouts  6.87 us (10%)
  between operations  2 us (3%)
    pallas_call x1, Pallas kernels, body(): pl.pallas_call(functools.partial(fused, nz, rows_b), out_shape=(jax.Shape...  62.3 us
    unnamed x19, local copies, waits for them, and re-layouts  6.36 us

profile of v1, /device:TPU:0, one launch (start us, length us, event | category | flops | bytes accessed | tf_op | source)
XLA Modules:
  0.0 71.2 jit_solution(7816010291352339536)
XLA Ops:
  0.6 0.0 copy-start.5
  1.9 0.8 %copy.16.pos = f32[1,3,2048]{2,1,0:T(4,128)S(1)} copy(f32[1,3,2048]{2,0,1:T(1,128)} %param.10) | data formatting | bytes 49152 | tf_op args[0]
  2.7 0.0 copy-done.5
  2.7 0.0 copy-start.1
  2.7 0.0 copy-start.2
  2.7 0.0 copy-start.3
  2.7 0.1 copy.17.w_out
  2.9 0.6 copy-done.1
  3.4 0.0 copy-done.2
  3.4 0.0 copy-done.3
  3.4 0.0 copy-start
  3.4 0.9 %copy-done = bf16[256,512]{1,0:T(8,128)(2,1)S(1)} copy-done((bf16[256,512]{1,0:T(8,128)(2,1)S(1)}, bf16[256,512]{1,0:T(8,128)(2,1)}, u32[]{:S(2)}) %copy-start) | copy-done | bytes 262168
  4.4 62.3 %shard_map.145 = (f32[1024,32]{1,0:T(8,128)S(1)}, f32[8,128]{1,0:T(8,128)S(1)}, f32[256,512]{1,0:T(8,128)S(1)}, f32[512,512]{1,0:T(8,128)}, f32[512,32]{1,0:T(8,128)S(1)}, /*index=5*/f32[8,512]{1,0:T(8,128)S(1)}) custom-call(f32[1,3,2048]{2,1,0:T(4,128)S(1)} %copy.16.pos, bf16[1,2048,256]{2,1,0:T(8,128)(2,1)} %feat.1, s32[1,2048]{1,0:T(1,128)S(1)} %copy-done.3, ...), custom_call_target="tpu_custom_call" | custom-call | tf_op jit(solution)/shard_map/pallas_call | solution.py:516
  66.7 0.0 copy-start.4
  66.7 0.5 slice.3
  67.3 0.8 %copy.18 = f32[1,1024,32]{1,2,0:T(8,128)} copy(f32[1,1024,32]{2,1,0:T(8,128)S(1)} %bitcast.2) | data formatting | bytes 262144
  68.1 0.7 %copy.19 = f32[512,32]{0,1:T(8,128)} copy(f32[512,32]{1,0:T(8,128)S(1)} %get-tuple-element.22) | data formatting | bytes 131072
  68.8 0.8 %copy.25 = f32[256,512]{1,0:T(8,128)} copy(f32[256,512]{1,0:T(8,128)S(1)} %get-tuple-element.32) | data formatting | bytes 1048576
  69.6 0.0 copy-done.4
  69.6 1.0 %copy.26 = f32[512,512]{1,0:T(8,128)} copy(f32[512,512]{1,0:T(8,128)S(1)} %copy-done.4) | data formatting | bytes 2097152
  70.6 0.6 copy.27
Async XLA Ops:
  0.6 2.1 %copy-start.5 = (bf16[512,32]{0,1:T(8,128)(2,1)S(1)}, bf16[512,32]{0,1:T(8,128)(2,1)}, u32[]{:S(2)}) copy-start(bf16[512,32]{0,1:T(8,128)(2,1)} %param.18) | copy-start | bytes 98308
  2.7 0.7 %copy-start.1 = (s32[3,1024]{1,0:T(4,128)S(1)}, s32[3,1024]{1,0:T(4,128)}, u32[]{:S(2)}) copy-start(s32[3,1024]{1,0:T(4,128)} %mill.1) | copy-start | bytes 36868
  2.7 0.7 %copy-start.2 = (f32[8,512]{1,0:T(8,128)S(1)}, f32[8,512]{1,0:T(8,128)}, u32[]{:S(2)}) copy-start(f32[8,512]{1,0:T(8,128)} %bias.1) | copy-start | bytes 49156
  2.7 0.7 %copy-start.3 = (s32[1,2048]{1,0:T(1,128)S(1)}, s32[1,2048]{1,0:T(1,128)}, u32[]{:S(2)}) copy-start(s32[1,2048]{1,0:T(1,128)} %spec.1) | copy-start | bytes 24580
  3.4 1.0 %copy-start = (bf16[256,512]{1,0:T(8,128)(2,1)S(1)}, bf16[256,512]{1,0:T(8,128)(2,1)}, u32[]{:S(2)}) copy-start(bf16[256,512]{1,0:T(8,128)(2,1)} %w_in.1) | copy-start | bytes 786436
  66.7 2.9 %copy-start.4 = (f32[512,512]{1,0:T(8,128)S(1)}, f32[512,512]{1,0:T(8,128)}, u32[]{:S(2)}) copy-start(f32[512,512]{1,0:T(8,128)} %get-tuple-element.33) | copy-start | bytes 3145732

commit v2 on v1

--- a/solution.py
+++ b/solution.py
@@ -193,23 +193,23 @@
 
 def fused(
     nz, rows_b,
-    pos, feat, spec, clen, eref, mill, w_in, w_mid, w_out, bias,
-    pot_o, en_o, gin_o, gmid_o, gout_o, gbias_o,
-    pos_f, pos_s, mill_f, mill_s, bias_f, bias_s, hot, out_t, cw,
+    pos, feat, spec, clen, eref, mill, w_in, w_mid, out_t, bias,
+    pot, en_o, all_0, all_1, all_2,
+    pos_f, pos_s, mill_f, mill_s, bias_f, bias_s, hot, cw,
     h1, h2, slope1, slope2, ch, turns, phases, panels,
     pz_s, pz_r, w_all, en_mine, en_z, en_x, en_sum,
-    pot, pot_s, pot_r, gc, g2, g1,
-    ga, ra_s, ra_r, xa_s, xa_r, za_s, za_r, all_a,
-    gb, rb_s, rb_r, xb_s, xb_r, zb_s, zb_r, all_b,
-    send, recv,
+    pot_s, pot_r, gc, g2, g1,
+    *rest,
 ):
+    send, recv = rest[-2:]
+    chunks = [(*rest[7 * c : 7 * c + 7], whole) for c, whole in enumerate((all_0, all_1, all_2))]
     z = lax.axis_index("atoms")
     x = lax.axis_index("kvec")
     r = lax.axis_index("rep")
     atoms = pos.shape[2]
     half = atoms // 2
     kv = mill.shape[1]
-    channels = w_out.shape[1]
+    channels = out_t.shape[0]
     width = 2 * kv // nz
     atoms_total = atoms * nz
     to_x = {"kvec": 1 - x}
@@ -239,9 +239,11 @@
     mill_f[...] = jnp.zeros_like(mill_f)
     bias_f[...] = jnp.zeros_like(bias_f)
     miller = mill[...].astype(F32)
-    for part, piece in enumerate(split_three(pos[0])):
-        pos_f[pl.ds(3 * part, 3), :] = piece
+    for part in range(3):
         mill_f[pl.ds(3 * part, 3), :] = miller
+    for axis in range(3):
+        for part, piece in enumerate(split_three(pos[axis])):
+            pos_f[pl.ds(3 * part + axis, 1), :] = piece
     pos_s[...] = pos_f[...].astype(BF)
     mill_s[...] = mill_f[...].astype(BF)
     for part, piece in enumerate(split_three(bias[...])):
@@ -250,11 +252,6 @@
     kinds = lax.rem(lax.broadcasted_iota(jnp.int32, hot.shape, 0), 16)
     own_kind = jnp.broadcast_to(spec[:, pl.ds(pl.multiple_of(x * half, 128), half)], hot.shape)
     hot[...] = (kinds == own_kind).astype(F32).astype(BF)
-    eye = (
-        lax.broadcasted_iota(jnp.int32, (channels, channels), 0)
-        == lax.broadcasted_iota(jnp.int32, (channels, channels), 1)
-    ).astype(F32).astype(BF)
-    out_t[...] = mul(eye, w_out[...], (1, 1)).astype(BF)
     factor = TWO_PI / jnp.full((1, kv), clen[0], F32)
     square = jnp.sum(miller * miller, axis=0, keepdims=True) * (factor * factor)
     decay = jnp.exp(-0.5 * square) / square * (1.0 / math.sqrt(atoms_total * KVECS))
@@ -279,34 +276,41 @@
         h2[at, :] = hidden
         ch[x, :, at] = mul(out_t[...], hidden, (1, 1)).astype(BF)
 
-    pl.semaphore_wait(barrier, len(peers))
-    charges = copy(ch.at[x], ch.at[x], to_x)
-
     panels[...] = jnp.zeros_like(panels)
+
+    def phase_tile(base):
+        turns[...] = mul(pos_s[:, pl.ds(base, ROWS)], mill_s[...], (0, 0))
+
+        @pl.loop(0, ROWS // STRIP, unroll=4)
+        def _(j):
+            near = turns[pl.ds(pl.multiple_of(j * STRIP, STRIP), STRIP), :]
+            near = near - ((near + TURN_SHIFT) - TURN_SHIFT)
+            sq = near * near
+            sine = near * (SINE[0] + sq * (SINE[1] + sq * (SINE[2] + sq * SINE[3])))
+            cosine = COSINE[0] + sq * (COSINE[1] + sq * (COSINE[2] + sq * (COSINE[3] + sq * COSINE[4])))
+            to = pl.ds(pl.multiple_of(base + j * STRIP, STRIP), STRIP)
+            phases[to, pl.ds(0, kv)] = (1.0 - sine * sine).astype(BF)
+            phases[to, pl.ds(kv, kv)] = (sine * cosine).astype(BF)
+
+    def panel_half(which):
+        @pl.loop(0, half // (2 * ROWS))
+        def _(i):
+            at = pl.ds(pl.multiple_of(i * 2 * ROWS, ROWS), 2 * ROWS)
+            base = pl.ds(pl.multiple_of(which * half + i * 2 * ROWS, ROWS), 2 * ROWS)
+            panels[...] += mul(ch[which, :, at], phases[base, :], (1, 0))
 
     def phase_half(which):
         @pl.loop(0, half // ROWS)
         def _(i):
-            at = pl.ds(pl.multiple_of(i * ROWS, ROWS), ROWS)
-            base = pl.multiple_of(which * half + i * ROWS, ROWS)
-            turns[...] = mul(pos_s[:, pl.ds(base, ROWS)], mill_s[...], (0, 0))
-
-            @pl.loop(0, ROWS // STRIP, unroll=4)
-            def _(j):
-                near = turns[pl.ds(pl.multiple_of(j * STRIP, STRIP), STRIP), :]
-                near = near - ((near + TURN_SHIFT) - TURN_SHIFT)
-                sq = near * near
-                sine = near * (SINE[0] + sq * (SINE[1] + sq * (SINE[2] + sq * SINE[3])))
-                cosine = COSINE[0] + sq * (COSINE[1] + sq * (COSINE[2] + sq * (COSINE[3] + sq * COSINE[4])))
-                to = pl.ds(pl.multiple_of(base + j * STRIP, STRIP), STRIP)
-                phases[to, pl.ds(0, kv)] = (1.0 - sine * sine).astype(BF)
-                phases[to, pl.ds(kv, kv)] = (sine * cosine).astype(BF)
-
-            panels[...] += mul(ch[which, :, at], phases[pl.ds(base, ROWS), :], (1, 0))
+            phase_tile(pl.multiple_of(which * half + i * ROWS, ROWS))
 
     phase_half(x)
+    pl.semaphore_wait(barrier, len(peers))
+    charges = copy(ch.at[x], ch.at[x], to_x)
+    panel_half(x)
+    phase_half(1 - x)
     charges.wait()
-    phase_half(1 - x)
+    panel_half(1 - x)
 
     def slab(who):
         return pl.ds(pl.multiple_of(who * width, 128), width)
@@ -323,17 +327,10 @@
     weighed = total * cw[:, slab(z)]
     w_all[z] = weighed.astype(BF)
     en_mine[...] = jnp.broadcast_to(jnp.sum(total * weighed).reshape(1, 1), en_mine.shape)
-    gathers = []
-    for step in range(1, nz):
-        gathers.append(copy(w_all.at[z], w_all.at[z], to_z(step)))
-        gathers.append(copy(en_mine, en_z.at[step], to_z(step)))
+    gathers = [copy(w_all.at[z], w_all.at[z], to_z(step)) for step in range(1, nz)]
+    shares = [copy(en_mine, en_z.at[step], to_z(step)) for step in range(1, nz)]
     for one in gathers:
         one.wait()
-    energy = en_mine[...]
-    for step in range(1, nz):
-        energy = energy + en_z[step]
-    en_sum[...] = energy
-    energies = copy(en_sum, en_x, to_x)
 
     def potential_half(which, store):
         @pl.loop(0, half // ROWS)
@@ -347,6 +344,13 @@
 
     potential_half(1 - x, pot_s)
     others = copy(pot_s, pot_r, to_x)
+    for one in shares:
+        one.wait()
+    energy = en_mine[...]
+    for step in range(1, nz):
+        energy = energy + en_z[step]
+    en_sum[...] = energy
+    energies = copy(en_sum, en_x, to_x)
     potential_half(x, pot)
     energies.wait()
     others.wait()
@@ -368,9 +372,6 @@
     def keep(store, first, value):
         for block in range(4):
             store[block, pl.ds(first, value.shape[0]), :] = value[:, block * lanes : (block + 1) * lanes]
-
-    for first in range(0, h1.shape[1], ROWS):
-        keep(ga, first, mul(h1[:, pl.ds(first, ROWS)], g2[...], (0, 0)))
 
     mine = 2 * r + x
 
@@ -406,7 +407,36 @@
         for one in made:
             one.wait()
 
-    rep_a = rep_start(ga, ra_s, ra_r)
+    def swap_pair(c):
+        g, out, into = chunks[c][:3]
+        return rep_start(g, out, into)
+
+    def swap_x(c):
+        g, _, got, out, into = chunks[c][:5]
+        return x_start(g, got, out, into)
+
+    def scatter(c):
+        g, _, got_r, _, got_x, out, into, _ = chunks[c]
+        return z_start(g, got_r, got_x, out, into)
+
+    def gather(c):
+        g, _, _, _, _, _, got, whole = chunks[c]
+        return z_gather(g, got, whole)
+
+    def gather_x(c):
+        whole = chunks[c][7]
+        return copy(whole.at[mine], whole.at[mine], to_x)
+
+    def gather_pair(c):
+        whole = chunks[c][7]
+        pair = pl.ds(2 * r, 2)
+        return copy(whole.at[pair], whole.at[pair], to_r)
+
+    part = h1.shape[1] // 2
+    keep(chunks[0][0], 0, mul(h1[:, pl.ds(0, part)], g2[...], (0, 0)))
+    pair_0 = swap_pair(0)
+    keep(chunks[1][0], 0, mul(h1[:, pl.ds(part, part)], g2[...], (0, 0)))
+    pair_1 = swap_pair(1)
 
     @pl.loop(0, half // ROWS)
     def _(i):
@@ -414,44 +444,60 @@
         back = mul(g2[at, :], w_mid[...], (1, 1))
         g1[at, :] = (back * slope1[at, :]).astype(BF)
 
-    rep_a.wait()
-    x_a = x_start(ga, ra_r, xa_s, xa_r)
+    pair_0.wait()
+    x_0 = swap_x(0)
+    pair_1.wait()
+    x_1 = swap_x(1)
     features_in = feat.shape[2]
     own = pl.ds(pl.multiple_of(x * half, ROWS), half)
-    gb[...] = jnp.zeros_like(gb)
-    keep(gb, 0, mul(feat[0, own, :], g1[...], (0, 0)))
-    keep(gb, features_in, mul(gc[...], h2[...], (1, 0)))
-    keep(gb, features_in + channels, mul(hot[pl.ds(0, 16), :], g1[...], (1, 0)))
-    rep_b = rep_start(gb, rb_s, rb_r)
-    x_a.wait()
-    z_a = z_start(ga, ra_r, xa_r, za_s, za_r)
-    rep_b.wait()
-    x_b = x_start(gb, rb_r, xb_s, xb_r)
-    pot_o[...] = pot[...].T
-    finish(z_a)
-    all_z_a = z_gather(ga, za_r, all_a)
-    x_b.wait()
-    z_b = z_start(gb, rb_r, xb_r, zb_s, zb_r)
-    finish(all_z_a)
-    all_x_a = copy(all_a.at[mine], all_a.at[mine], to_x)
-    finish(z_b)
-    all_z_b = z_gather(gb, zb_r, all_b)
-    all_x_a.wait()
-    pair = pl.ds(2 * r, 2)
-    all_r_a = copy(all_a.at[pair], all_a.at[pair], to_r)
-    finish(all_z_b)
-    all_x_b = copy(all_b.at[mine], all_b.at[mine], to_x)
-    all_r_a.wait()
+    last = chunks[2][0]
+    last[...] = jnp.zeros_like(last)
+    keep(last, 0, mul(feat[0, own, :], g1[...], (0, 0)))
+    keep(last, features_in, mul(gc[...], h2[...], (1, 0)))
+    keep(last, features_in + channels, mul(hot[pl.ds(0, 16), :], g1[...], (1, 0)))
+    pair_2 = swap_pair(2)
+    x_0.wait()
+    z_0 = scatter(0)
+    pair_2.wait()
+    x_2 = swap_x(2)
+    x_1.wait()
+    z_1 = scatter(1)
+    finish(z_0)
+    gz_0 = gather(0)
+    x_2.wait()
+    z_2 = scatter(2)
+    finish(z_1)
+    gz_1 = gather(1)
+    finish(gz_0)
+    gx_0 = gather_x(0)
+    finish(z_2)
+    gz_2 = gather(2)
+    finish(gz_1)
+    gx_1 = gather_x(1)
+    gx_0.wait()
+    gr_0 = gather_pair(0)
+    finish(gz_2)
+    gx_2 = gather_x(2)
+    gx_1.wait()
+    gr_1 = gather_pair(1)
+    gx_2.wait()
+    gr_2 = gather_pair(2)
+    finish([gr_0, gr_1, gr_2])
+
+
+def write(features_in, pot, energy, all_0, all_1, all_2, pot_o, en_o, gin_o, gmid_o, gout_o, gbias_o):
+    channels = pot.shape[0]
+    part = all_0.shape[1]
+    en_o[0] = energy[0, 0]
+    pot_o[0] = pot[...]
     for block in range(4):
-        gmid_o[:, pl.ds(block * lanes, lanes)] = all_a[block].astype(F32)
-    all_x_b.wait()
-    all_r_b = copy(all_b.at[pair], all_b.at[pair], to_r)
-    all_r_b.wait()
-    for block in range(4):
-        at = pl.ds(block * lanes, lanes)
-        gin_o[:, at] = all_b[block, pl.ds(0, features_in), :].astype(F32)
-        gout_o[at, :] = all_b[block, pl.ds(features_in, channels), :].astype(F32).T
-        gbias_o[:, at] = all_b[block, pl.ds(features_in + channels, 16), :].astype(F32)[: gbias_o.shape[0]]
+        at = pl.ds(block * 128, 128)
+        gmid_o[pl.ds(0, part), at] = all_0[block].astype(F32)
+        gmid_o[pl.ds(part, part), at] = all_1[block].astype(F32)
+        gin_o[:, at] = all_2[block, pl.ds(0, features_in), :].astype(F32)
+        gout_o[:, at] = all_2[block, pl.ds(features_in, channels), :].astype(F32)
+        bias_rows = all_2[block, pl.ds(features_in + channels, 16), :].astype(F32)
+        gbias_o[:, at] = bias_rows[: gbias_o.shape[0]]
 
 
 def fits(sizes, args):
@@ -463,7 +509,7 @@
         and nz > 1
         and (2 * kv) % (128 * nz) == 0
         and atoms % (2 * ROWS) == 0
-        and args[7].shape[0] % (16 * nz) == 0
+        and args[7].shape[0] % (32 * nz) == 0
         and args[7].shape[1] == 512
         and args[9].shape[0] <= 16
     )
@@ -479,7 +525,7 @@
     width = 2 * kv // nz
     inner, channels = weight_out.shape
     features_in = features.shape[2]
-    rows_a = inner
+    rows_a = inner // 2
     rows_b = -(-(features_in + channels + 16) // (16 * nz)) * 16 * nz
 
     def vmem(*shape, dtype=F32):
@@ -491,14 +537,13 @@
             vmem(2, rows, 128, dtype=BF), vmem(2, rows, 128, dtype=BF),
             vmem(rows, 128, dtype=BF), vmem(rows, 128, dtype=BF),
             vmem(rows, 128, dtype=BF), vmem(nz, rows // nz, 128, dtype=BF),
-            vmem(4, rows, 128, dtype=BF),
         ]
 
     scratch = [
         vmem(16, atoms), vmem(16, atoms, dtype=BF),
         vmem(16, kv), vmem(16, kv, dtype=BF),
         vmem(48, inner), vmem(48, inner, dtype=BF),
-        vmem(48, half, dtype=BF), vmem(channels, inner, dtype=BF), vmem(1, 2 * kv),
+        vmem(48, half, dtype=BF), vmem(1, 2 * kv),
         vmem(half, inner, dtype=BF), vmem(half, inner, dtype=BF),
         vmem(half, inner), vmem(half, inner),
         vmem(2, channels, half, dtype=BF), vmem(ROWS, kv), vmem(atoms, 2 * kv, dtype=BF),
@@ -506,31 +551,46 @@
         vmem(nz, channels, width, dtype=BF), vmem(nz, channels, width, dtype=BF),
         vmem(nz, channels, width, dtype=BF),
         vmem(8, 128), vmem(nz, 8, 128), vmem(8, 128), vmem(8, 128),
-        vmem(channels, half), vmem(channels, half, dtype=BF), vmem(channels, half, dtype=BF),
+        vmem(channels, half, dtype=BF), vmem(channels, half, dtype=BF),
         vmem(channels, half, dtype=BF), vmem(half, inner, dtype=BF), vmem(half, inner, dtype=BF),
-        *grads(rows_a), *grads(rows_b),
-        pltpu.SemaphoreType.DMA((48,)), pltpu.SemaphoreType.DMA((48,)),
+        *grads(rows_a), *grads(rows_a), *grads(rows_b),
+        pltpu.SemaphoreType.DMA((56,)), pltpu.SemaphoreType.DMA((56,)),
     ]
     place = pl.BlockSpec(memory_space=pltpu.VMEM)
     scalar = pl.BlockSpec(memory_space=pltpu.SMEM)
-    potential, energy, grad_in, grad_mid, grad_out, grad_bias = pl.pallas_call(
+    found = pl.pallas_call(
         functools.partial(fused, nz, rows_b),
         out_shape=(
-            jax.ShapeDtypeStruct((half, channels), F32),
+            jax.ShapeDtypeStruct((channels, half), F32),
             jax.ShapeDtypeStruct((8, 128), F32),
-            jax.ShapeDtypeStruct((features_in, inner), F32),
-            jax.ShapeDtypeStruct((inner, inner), F32),
-            jax.ShapeDtypeStruct((inner, channels), F32),
-            jax.ShapeDtypeStruct(species_bias.shape, F32),
+            jax.ShapeDtypeStruct((4, rows_a, 128), BF),
+            jax.ShapeDtypeStruct((4, rows_a, 128), BF),
+            jax.ShapeDtypeStruct((4, rows_b, 128), BF),
         ),
         in_specs=[place, place, place, scalar, scalar] + [place] * 5,
-        out_specs=[place] * 6,
+        out_specs=[place] * 5,
         scratch_shapes=scratch,
         compiler_params=pltpu.CompilerParams(
             collective_id=0, has_side_effects=True, vmem_limit_bytes=52 * 2**20
         ),
-    )(*args)
-    return (potential[None], energy[0, :1], grad_in, grad_mid, grad_out, grad_bias)
+    )(jnp.swapaxes(positions, 0, 1), *args[1:8], weight_out.T, species_bias)
+    potential, energy, grad_in, grad_mid, grad_out, grad_bias = (
+        pl.pallas_call(
+            functools.partial(write, features_in),
+            out_shape=(
+                jax.ShapeDtypeStruct((1, channels, half), F32),
+                jax.ShapeDtypeStruct((1,), F32),
+                jax.ShapeDtypeStruct((features_in, inner), F32),
+                jax.ShapeDtypeStruct((inner, inner), F32),
+                jax.ShapeDtypeStruct((channels, inner), F32),
+                jax.ShapeDtypeStruct(species_bias.shape, F32),
+            ),
+            in_specs=[place] * 5,
+            out_specs=[place, scalar] + [place] * 4,
+            compiler_params=pltpu.CompilerParams(vmem_limit_bytes=16 * 2**20),
+        )(*found)
+    )
+    return (jnp.swapaxes(potential, 1, 2), energy, grad_in, grad_mid, grad_out.T, grad_bias)
 
 
 def solution(mesh):

time: 71.6 us -> 68.1 us (0.951)
  Pallas kernels: 62.3 us -> 60 us
  local copies, waits for them, and re-layouts: 6.87 us -> 5.61 us
    pallas_call x1, Pallas kernels: 62.3 us -> 58.7 us  [body(): pl.pallas_call(functools.partial(fused, nz, rows_b), out_shape=(jax.Shape...]
    pallas_call x0 -> x1, Pallas kernels: none -> 1.29 us  [body(): pl.pallas_call(functools.partial(write, features_in), out_shape=(jax.Shap...]
    unnamed x19 -> x14, local copies, waits for them, and re-layouts: 6.36 us -> 5.61 us
where the time goes in v2:
time: 68.1 us; the launch traced here: 67.6 us
  Pallas kernels  60 us (88%)
  local copies, waits for them, and re-layouts  5.61 us (8%)
  between operations  1.95 us (3%)
    pallas_call x1, Pallas kernels, body(): pl.pallas_call(functools.partial(fused, nz, rows_b), out_shape=(jax.Shape...  58.7 us
    unnamed x14, local copies, waits for them, and re-layouts  5.61 us

profile of v2, /device:TPU:0, one launch (start us, length us, event | category | flops | bytes accessed | tf_op | source)
XLA Modules:
  0.0 67.6 jit_solution(13658120871161675320)
XLA Ops:
  1.9 0.0 copy-start
  1.9 1.0 %copy-done = bf16[512,512]{1,0:T(8,128)(2,1)S(1)} copy-done((bf16[512,512]{1,0:T(8,128)(2,1)S(1)}, bf16[512,512]{1,0:T(8,128)(2,1)}, u32[]{:S(2)}) %copy-start) | copy-done | bytes 524312
  3.0 0.0 copy-start.1
  3.0 0.9 %copy-done.1 = bf16[256,512]{1,0:T(8,128)(2,1)S(1)} copy-done((bf16[256,512]{1,0:T(8,128)(2,1)S(1)}, bf16[256,512]{1,0:T(8,128)(2,1)}, u32[]{:S(2)}) %copy-start.1) | copy-done | bytes 262168
  3.9 0.0 copy-start.2
  3.9 0.8 %copy-done.2 = bf16[512,32]{0,1:T(8,128)(2,1)S(1)} copy-done((bf16[512,32]{0,1:T(8,128)(2,1)S(1)}, bf16[512,32]{0,1:T(8,128)(2,1)}, u32[]{:S(2)}) %copy-start.2) | copy-done | bytes 32792
  4.7 0.0 copy-start.3
  4.7 0.7 %copy-done.3 = f32[1,3,2048]{2,0,1:T(1,128)S(1)} copy-done((f32[1,3,2048]{2,0,1:T(1,128)S(1)}, f32[1,3,2048]{2,0,1:T(1,128)}, u32[]{:S(2)}) %copy-start.3) | copy-done | bytes 24600
  5.4 0.0 copy-start.4
  5.4 0.7 %copy-done.4 = s32[3,1024]{1,0:T(4,128)S(1)} copy-done((s32[3,1024]{1,0:T(4,128)S(1)}, s32[3,1024]{1,0:T(4,128)}, u32[]{:S(2)}) %copy-start.4) | copy-done | bytes 12312
  6.1 0.0 copy-start.5
  6.1 0.7 %copy-done.5 = f32[8,512]{1,0:T(8,128)S(1)} copy-done((f32[8,512]{1,0:T(8,128)S(1)}, f32[8,512]{1,0:T(8,128)}, u32[]{:S(2)}) %copy-start.5) | copy-done | bytes 16408
  6.9 0.0 copy-start.6
  6.9 0.7 %copy-done.6 = s32[1,2048]{1,0:T(1,128)S(1)} copy-done((s32[1,2048]{1,0:T(1,128)S(1)}, s32[1,2048]{1,0:T(1,128)}, u32[]{:S(2)}) %copy-start.6) | copy-done | bytes 8216
  7.5 58.7 %shard_map.145 = (f32[32,1024]{1,0:T(8,128)S(1)}, f32[8,128]{1,0:T(8,128)S(1)}, bf16[4,256,128]{2,1,0:T(8,128)(2,1)S(1)}, bf16[4,256,128]{2,1,0:T(8,128)(2,1)S(1)}, bf16[4,320,128]{2,1,0:T(8,128)(2,1)S(1)}) custom-call(f32[3,1,2048]{2,1,0:T(1,128)S(1)} %bitcast.5, bf16[1,2048,256]{2,1,0:T(8,128)(2,1)} %feat.1, s32[1,2048]{1,0:T(1,128)S(1)} %copy-done.6, ...), custom_call_target="tpu_custom_call" | custom-call | tf_op jit(solution)/shard_map/pallas_call | solution.py:561
  66.3 1.3 %shard_map.146 = (f32[1,32,1024]{2,1,0:T(8,128)}, f32[1]{0:T(128)}, f32[256,512]{1,0:T(8,128)}, f32[512,512]{1,0:T(8,128)}, f32[32,512]{1,0:T(8,128)}, /*index=5*/f32[8,512]{1,0:T(8,128)}) custom-call(f32[32,1024]{1,0:T(8,128)S(1)} %get-tuple-element.17.pot, f32[8,128]{1,0:T(8,128)S(1)} %get-tuple-element.18.energy, ...), custom_call_target="tpu_custom_call" | custom-call | tf_op jit(solution)/shard_map/pallas_call | solution.py:578
Async XLA Ops:
  1.9 1.0 %copy-start = (bf16[512,512]{1,0:T(8,128)(2,1)S(1)}, bf16[512,512]{1,0:T(8,128)(2,1)}, u32[]{:S(2)}) copy-start(bf16[512,512]{1,0:T(8,128)(2,1)} %w_mid.1) | copy-start | bytes 1572868
  3.0 0.9 %copy-start.1 = (bf16[256,512]{1,0:T(8,128)(2,1)S(1)}, bf16[256,512]{1,0:T(8,128)(2,1)}, u32[]{:S(2)}) copy-start(bf16[256,512]{1,0:T(8,128)(2,1)} %w_in.1) | copy-start | bytes 786436
  3.9 0.8 %copy-start.2 = (bf16[512,32]{0,1:T(8,128)(2,1)S(1)}, bf16[512,32]{0,1:T(8,128)(2,1)}, u32[]{:S(2)}) copy-start(bf16[512,32]{0,1:T(8,128)(2,1)} %param.18) | copy-start | bytes 98308
  4.7 0.7 %copy-start.3 = (f32[1,3,2048]{2,0,1:T(1,128)S(1)}, f32[1,3,2048]{2,0,1:T(1,128)}, u32[]{:S(2)}) copy-start(f32[1,3,2048]{2,0,1:T(1,128)} %param.10) | copy-start | bytes 73732
  5.4 0.7 %copy-start.4 = (s32[3,1024]{1,0:T(4,128)S(1)}, s32[3,1024]{1,0:T(4,128)}, u32[]{:S(2)}) copy-start(s32[3,1024]{1,0:T(4,128)} %mill.1) | copy-start | bytes 36868
  6.1 0.7 %copy-start.5 = (f32[8,512]{1,0:T(8,128)S(1)}, f32[8,512]{1,0:T(8,128)}, u32[]{:S(2)}) copy-start(f32[8,512]{1,0:T(8,128)} %bias.1) | copy-start | bytes 49156
  6.9 0.7 %copy-start.6 = (s32[1,2048]{1,0:T(1,128)S(1)}, s32[1,2048]{1,0:T(1,128)}, u32[]{:S(2)}) copy-start(s32[1,2048]{1,0:T(1,128)} %spec.1) | copy-start | bytes 24580

commit v3 on v2

--- a/solution.py
+++ b/solution.py
@@ -193,20 +193,21 @@
 
 def fused(
     nz, rows_b,
-    pos, feat, spec, clen, eref, mill, w_in, w_mid, out_t, bias,
+    pos_h, feat_h, spec_h, clen, eref, mill_h, w_in_h, w_mid_h, out_h, bias_h,
     pot, en_o, all_0, all_1, all_2,
+    pos, feat, spec, mill, w_in, w_mid, out_t, bias,
     pos_f, pos_s, mill_f, mill_s, bias_f, bias_s, hot, cw,
     h1, h2, slope1, slope2, ch, turns, phases, panels,
     pz_s, pz_r, w_all, en_mine, en_z, en_x, en_sum,
     pot_s, pot_r, gc, g2, g1,
     *rest,
 ):
-    send, recv = rest[-2:]
+    send, recv, load = rest[-3:]
     chunks = [(*rest[7 * c : 7 * c + 7], whole) for c, whole in enumerate((all_0, all_1, all_2))]
     z = lax.axis_index("atoms")
     x = lax.axis_index("kvec")
     r = lax.axis_index("rep")
-    atoms = pos.shape[2]
+    atoms = pos_h.shape[2]
     half = atoms // 2
     kv = mill.shape[1]
     channels = out_t.shape[0]
@@ -218,10 +219,19 @@
     def to_z(step):
         return {"atoms": lax.rem(z + step, nz)}
 
+    own_rows = pl.ds(pl.multiple_of(x * half, ROWS), half)
+    pairs = (
+        (pos_h, pos), (mill_h, mill), (bias_h, bias), (spec_h, spec),
+        (feat_h.at[0, own_rows], feat), (w_in_h, w_in), (w_mid_h, w_mid), (out_h, out_t),
+    )
+    loads = [pltpu.make_async_copy(src, dst, load.at[i]) for i, (src, dst) in enumerate(pairs)]
     barrier = pltpu.get_barrier_semaphore()
     peers = [to_x, to_r] + [to_z(step) for step in range(1, nz)]
     for peer in peers:
         pl.semaphore_signal(barrier, inc=1, device_id=peer, device_id_type=pl.DeviceIdType.MESH)
+
+    for one in loads:
+        one.start()
 
     count = [0]
 
@@ -234,6 +244,9 @@
         )
         made.start()
         return made
+
+    for one in loads[:4]:
+        one.wait()
 
     pos_f[...] = jnp.zeros_like(pos_f)
     mill_f[...] = jnp.zeros_like(mill_f)
@@ -258,11 +271,13 @@
     cw[:, pl.ds(0, kv)] = decay
     cw[:, pl.ds(kv, kv)] = decay
 
+    for one in loads[4:]:
+        one.wait()
+
     @pl.loop(0, half // ROWS)
     def _(i):
         at = pl.ds(pl.multiple_of(i * ROWS, ROWS), ROWS)
-        source = pl.ds(pl.multiple_of(x * half + i * ROWS, ROWS), ROWS)
-        linear = mul(feat[0, source, :], w_in[...], (1, 0)) + mul(hot[:, at], bias_s[...], (0, 0))
+        linear = mul(feat[at, :], w_in[...], (1, 0)) + mul(hot[:, at], bias_s[...], (0, 0))
         gate = 0.5 * jnp.tanh(0.5 * linear) + 0.5
         hidden = linear * gate
         slope1[at, :] = gate + hidden * (1.0 - gate)
@@ -448,11 +463,10 @@
     x_0 = swap_x(0)
     pair_1.wait()
     x_1 = swap_x(1)
-    features_in = feat.shape[2]
-    own = pl.ds(pl.multiple_of(x * half, ROWS), half)
+    features_in = feat.shape[1]
     last = chunks[2][0]
     last[...] = jnp.zeros_like(last)
-    keep(last, 0, mul(feat[0, own, :], g1[...], (0, 0)))
+    keep(last, 0, mul(feat[...], g1[...], (0, 0)))
     keep(last, features_in, mul(gc[...], h2[...], (1, 0)))
     keep(last, features_in + channels, mul(hot[pl.ds(0, 16), :], g1[...], (1, 0)))
     pair_2 = swap_pair(2)
@@ -540,6 +554,9 @@
         ]
 
     scratch = [
+        vmem(3, 1, atoms), vmem(half, features_in, dtype=BF), vmem(1, atoms, dtype=jnp.int32),
+        vmem(3, kv, dtype=jnp.int32), vmem(features_in, inner, dtype=BF), vmem(inner, inner, dtype=BF),
+        vmem(channels, inner, dtype=BF), vmem(*species_bias.shape),
         vmem(16, atoms), vmem(16, atoms, dtype=BF),
         vmem(16, kv), vmem(16, kv, dtype=BF),
         vmem(48, inner), vmem(48, inner, dtype=BF),
@@ -554,10 +571,11 @@
         vmem(channels, half, dtype=BF), vmem(channels, half, dtype=BF),
         vmem(channels, half, dtype=BF), vmem(half, inner, dtype=BF), vmem(half, inner, dtype=BF),
         *grads(rows_a), *grads(rows_a), *grads(rows_b),
-        pltpu.SemaphoreType.DMA((56,)), pltpu.SemaphoreType.DMA((56,)),
+        pltpu.SemaphoreType.DMA((56,)), pltpu.SemaphoreType.DMA((56,)), pltpu.SemaphoreType.DMA((8,)),
     ]
     place = pl.BlockSpec(memory_space=pltpu.VMEM)
     scalar = pl.BlockSpec(memory_space=pltpu.SMEM)
+    stay = pl.BlockSpec(memory_space=pltpu.HBM)
     found = pl.pallas_call(
         functools.partial(fused, nz, rows_b),
         out_shape=(
@@ -567,11 +585,11 @@
             jax.ShapeDtypeStruct((4, rows_a, 128), BF),
             jax.ShapeDtypeStruct((4, rows_b, 128), BF),
         ),
-        in_specs=[place, place, place, scalar, scalar] + [place] * 5,
+        in_specs=[stay, stay, stay, scalar, scalar] + [stay] * 5,
         out_specs=[place] * 5,
         scratch_shapes=scratch,
         compiler_params=pltpu.CompilerParams(
-            collective_id=0, has_side_effects=True, vmem_limit_bytes=52 * 2**20
+            collective_id=0, has_side_effects=True, vmem_limit_bytes=60 * 2**20
         ),
     )(jnp.swapaxes(positions, 0, 1), *args[1:8], weight_out.T, species_bias)
     potential, energy, grad_in, grad_mid, grad_out, grad_bias = (
@@ -587,7 +605,7 @@
             ),
             in_specs=[place] * 5,
             out_specs=[place, scalar] + [place] * 4,
-            compiler_params=pltpu.CompilerParams(vmem_limit_bytes=16 * 2**20),
+            compiler_params=pltpu.CompilerParams(vmem_limit_bytes=60 * 2**20),
         )(*found)
     )
     return (jnp.swapaxes(potential, 1, 2), energy, grad_in, grad_mid, grad_out.T, grad_bias)

time: 68.1 us -> 64.4 us (0.946)
  local copies, waits for them, and re-layouts: 5.61 us -> 0 us
  Pallas kernels: 60 us -> 62.3 us
    unnamed x14 -> x0, local copies, waits for them, and re-layouts: 5.61 us -> none
    pallas_call x1, Pallas kernels: 1.29 us -> 2.49 us  [body(): pl.pallas_call(functools.partial(write, features_in), out_shape=(jax.Shap...]
    pallas_call x1, Pallas kernels: 58.7 us -> 59.8 us  [body(): pl.pallas_call(functools.partial(fused, nz, rows_b), out_shape=(jax.Shape...]
where the time goes in v3:
time: 64.4 us; the launch traced here: 64.2 us
  Pallas kernels  62.3 us (97%)
  between operations  1.93 us (3%)
    pallas_call x1, Pallas kernels, body(): pl.pallas_call(functools.partial(fused, nz, rows_b), out_shape=(jax.Shape...  59.8 us
    pallas_call x1, Pallas kernels, body(): pl.pallas_call(functools.partial(write, features_in), out_shape=(jax.Shap...  2.49 us

profile of v3, /device:TPU:0, one launch (start us, length us, event | category | flops | bytes accessed | tf_op | source)
XLA Modules:
  0.0 64.2 jit_solution(149100780640554414)
XLA Ops:
  1.9 59.8 %shard_map.145 = (f32[32,1024]{1,0:T(8,128)}, f32[8,128]{1,0:T(8,128)}, bf16[4,256,128]{2,1,0:T(8,128)(2,1)}, bf16[4,256,128]{2,1,0:T(8,128)(2,1)}, bf16[4,320,128]{2,1,0:T(8,128)(2,1)}) custom-call(f32[3,1,2048]{2,1,0:T(1,128)} %bitcast.5, bf16[1,2048,256]{2,1,0:T(8,128)(2,1)} %feat_h.1, s32[1,2048]{1,0:T(1,128)} %spec_h.1, f32[1]{0:T(128)S(6)} %copy.16.clen, ...), custom_call_target="tpu_custom_call" | custom-call | tf_op jit(solution)/shard_map/pallas_call | solution.py:579
  61.7 2.5 %shard_map.146 = (f32[1,32,1024]{2,1,0:T(8,128)}, f32[1]{0:T(128)}, f32[256,512]{1,0:T(8,128)}, f32[512,512]{1,0:T(8,128)}, f32[32,512]{1,0:T(8,128)}, /*index=5*/f32[8,512]{1,0:T(8,128)}) custom-call(f32[32,1024]{1,0:T(8,128)} %get-tuple-element.17.pot, f32[8,128]{1,0:T(8,128)} %get-tuple-element.18.energy, bf16[4,256,128]{2,1,0:T(8,128)(2,1)} %get-tuple-element.19.all_0, ...), custom_call_target="tpu_custom_call" | custom-call | tf_op jit(solution)/shard_map/pallas_call | solution.py:596
